TPU v7x, 32 devices: a whole 2x2x4 slice. The times are simulated.
32 devices in a mesh: groups: 2 (over x), blk: 16 (over z, y, core).
Axes of the slice: x: 2, y: 2, z: 4, core: 2. Of those that a mesh axis runs over, the one named last changes fastest.
Arguments:
- environments: bfloat16 [40960, 4096], P(('groups', 'blk')), parts along dimension 0, may hold values from -40 to 40
- targets: bfloat16 [3, 40960], P(None, ('groups', 'blk')), parts along dimension 1, may hold values from -1 to 3
- sparse_points: bfloat16 [128, 4096], P(('groups', 'blk')), parts along dimension 0, may hold values from -0.09375 to 0.09375
- block_pair: int32 [2560], P(('groups', 'blk')), parts along dimension 0, may hold values from 0 to 7
- coupling: int32 [8, 8], replicated, may hold values from 0 to 1, as said below
Outputs:
- gram: float32 [128, 64], P(('groups', 'blk')), parts along dimension 0
- projected: float32 [3, 128], P(None, ('groups', 'blk')), parts along dimension 1
There are 2 independent parts, one for each index of `groups`. A program takes and returns all parts, laid end to end along the dimension named above; an argument that names none is the same for every part. Nothing has to cross between parts.
Inputs may be any that keep to these rules, and one draw needn't show every extreme that they name: coupling[p, p] is 1 for every p.
All inputs are finite; a program needn't handle non-finite values.
Results may differ from a plain program's by a relative error of at most 0.0003.
Values may be sent and summed in bfloat16 or wider, within the bound.
A program may use at most 64 MiB of HBM per device.

v0:
```python
import jax
import jax.numpy as jnp
from jax import lax
from jax.sharding import PartitionSpec as P

EBLK = 16
PAIRS = 8


def shards(environments, targets, sparse_points, block_pair, coupling):
    rows = environments.shape[0]
    devices = lax.axis_size("blk")
    total = rows * devices
    pts_dev = sparse_points.shape[0]
    points = pts_dev * devices
    per_pair = points // PAIRS
    labels = jnp.arange(PAIRS, dtype=jnp.int32)
    env_pair = jnp.repeat(block_pair, EBLK)
    env_onehot = (env_pair[:, None] == labels[None, :]).astype(jnp.float32)
    env_links = jnp.dot(env_onehot, coupling.astype(jnp.float32))
    piece = lax.all_gather(sparse_points, "blk", axis=0, tiled=True)
    col_pair = jnp.arange(piece.shape[0], dtype=jnp.int32) // per_pair
    col_onehot = (col_pair[:, None] == labels[None, :]).astype(jnp.float32)
    mask = jnp.dot(env_links, col_onehot.T)
    dots = lax.dot_general(
        environments, piece, (((1,), (1,)), ((), ())), preferred_element_type=jnp.float32
    )
    kernel = (mask * dots * dots).astype(jnp.bfloat16)
    own_gram = lax.psum_scatter(
        lax.dot_general(
            kernel, kernel, (((0,), (0,)), ((), ())), preferred_element_type=jnp.float32
        ),
        "blk",
        scatter_dimension=0,
        tiled=True,
    )
    proj_all = jnp.dot(targets, kernel, preferred_element_type=jnp.float32)
    own_proj = lax.psum_scatter(proj_all, "blk", scatter_dimension=1, tiled=True)
    return (own_gram / total, own_proj / total)


def solution(mesh):
    in_specs = (
        P(("groups", "blk"), None),
        P(None, ("groups", "blk")),
        P(("groups", "blk"), None),
        P(("groups", "blk")),
        P(),
    )
    out_specs = (P(("groups", "blk"), None), P(None, ("groups", "blk")))
    return jax.shard_map(shards, mesh=mesh, in_specs=in_specs, out_specs=out_specs, check_vma=False)
```

profile of v0, /device:TPU:0, one launch (start us, length us, event | category | flops | bytes accessed | tf_op | source)
XLA Modules:
  0.0 94.2 jit_solution(13968776519205026309)
XLA Ops:
  0.6 0.0 copy-start
  0.6 0.0 copy-start.3
  0.7 0.0 copy-start.2
  0.7 0.0 copy-start.1
  0.7 24.8 %all-gather = bf16[16,4,4096]{2,1,0:T(4,128)(2,1)S(1)} all-gather(bf16[1,4,4096]{2,1,0:T(4,128)(2,1)} %bitcast.12), channel_id=1, replica_groups=mesh['groups'=2,'blk'=16] {'blk'}, dimensions={0}, use_global_device_ids=true | all-gather | bytes 557056 | tf_op jit(solution)/shard_map/all_gather | solution.py:21
  25.5 0.1 reshape.19
  25.6 7.3 %fusion.9 = f32[1280,64]{0,1:T(8,128)S(1)} fusion(bf16[1280,4096]{1,0:T(8,128)(2,1)} %param.5, bf16[64,4096]{1,0:T(8,128)(2,1)S(1)} %reshape.19), kind=kOutput, calls=%fused_computation.16 | convolution fusion | flops 671088640 | bytes 11337728 | tf_op jit(solution)/shard_map/dot_general | solution.py:25
  32.9 0.0 copy-done.2
  32.9 0.1 broadcast_in_dim.2
  33.0 0.1 eq.28
  33.1 0.0 copy-done.1
  33.1 0.5 fusion.1
  33.6 0.2 fusion.10
  33.8 0.0 copy-done
  33.8 0.1 convolution_bitcast_fusion
  33.9 57.9 %all-reduce.2 = (f32[64,64]{1,0:T(8,128)S(1)}, f32[3,64]{1,0:T(4,128)S(1)}) all-reduce(f32[64,64]{1,0:T(8,128)S(1)} %fusion.10, f32[3,64]{1,0:T(4,128)S(1)} %convolution_bitcast_fusion), channel_id=2, replica_groups=mesh['groups'=2,'blk'=16] {'blk'}, use_global_device_ids=true, to_apply=%region_0.1.clone | all-reduce | flops 4288 | bytes 34304
  91.8 0.0 copy-done.3
  91.8 0.6 dynamic-slice
  93.0 0.7 dynamic-slice_multiply_fusion
  93.7 0.6 dynamic-slice_multiply_fusion.1
  (1 shorter events, 0.0 us)
Async XLA Ops:
  0.6 33.1 %copy-start = (bf16[3,1280]{1,0:T(4,128)(2,1)S(1)}, bf16[3,1280]{1,0:T(4,128)(2,1)}, u32[]{:S(2)}) copy-start(bf16[3,1280]{1,0:T(4,128)(2,1)} %param.6) | copy-start | bytes 23044
  0.6 91.1 %copy-start.3 = (u32[32]{0:T(128)S(1)}, u32[32]{0:T(128)}, u32[]{:S(2)}) copy-start(u32[32]{0:T(128)} %constant.27) | copy-start | bytes 388
  0.7 32.2 %copy-start.2 = (s32[80]{0:T(128)S(1)}, s32[80]{0:T(128)}, u32[]{:S(2)}) copy-start(s32[80]{0:T(128)} %param.8) | copy-start | bytes 964
  0.7 32.4 %copy-start.1 = (s32[8,8]{1,0:T(8,128)S(1)}, s32[8,8]{1,0:T(8,128)}, u32[]{:S(2)}) copy-start(s32[8,8]{1,0:T(8,128)} %param.9) | copy-start | bytes 772
where the time goes:
time: 94.5 us; the launch traced here: 94.2 us
  blocking collectives  82.7 us (88%)
  matrix products  8.1 us (9%)
  between operations  1.36 us (1%)
  other arithmetic  1.24 us (1%)
    unnamed x1, blocking collectives  57.9 us
    all_gather x1, blocking collectives, shards(): piece = lax.all_gather(sparse_points, 'blk', axis=0, tiled=True)  24.8 us
    dot_general x1, matrix products, shards(): lax.dot_general(environments, piece, (((1,), (1,)), ((), ())), preferred_...  7.28 us

commit v1 on v0

v1 whole, which is shorter than its diff:
```python
import functools

import jax
import jax.numpy as jnp
from jax import lax
from jax.experimental import pallas as pl
from jax.experimental.pallas import tpu as pltpu
from jax.sharding import PartitionSpec as P

EBLK = 16
PAIRS = 8
LANES = 128
CHUNKS = 4
MESH = pl.DeviceIdType.MESH


def grid_of(devices):
    chips = devices // 2
    inner = 1
    while (inner * 2) ** 2 <= chips and chips % (inner * 2) == 0:
        inner *= 2
    return chips // inner, inner


def kernel(
    n,
    env_hbm,
    tgt_hbm,
    pts_hbm,
    pair_hbm,
    coup_hbm,
    out_ref,
    env,
    tgt,
    pair,
    coup,
    gathered,
    acc,
    part,
    landed,
    env_sem,
    small_sem,
    own_sem,
    send_sem,
    recv_sem,
    part_send,
    part_recv,
):
    outer, inner = grid_of(n)
    group = lax.axis_index("groups")
    me = lax.axis_index("blk")
    core = me % 2
    row = (me // 2) // inner
    col = (me // 2) % inner
    rows = env_hbm.shape[0]
    width = env_hbm.shape[1] // CHUNKS
    piece = pts_hbm.shape[0] // CHUNKS
    tiles = width // LANES
    pts_dev = pts_hbm.shape[0] * LANES // env_hbm.shape[1]
    points = pts_dev * n
    per_pair = points // PAIRS
    heads = tgt_hbm.shape[0]
    blocks = rows // EBLK

    def index(r, c, k):
        return (r * inner + c) * 2 + k

    loads = [
        pltpu.make_async_copy(env_hbm.at[:, pl.ds(c * width, width)], env.at[c], env_sem.at[c])
        for c in range(CHUNKS)
    ]
    small = [
        pltpu.make_async_copy(src, dst, small_sem.at[i])
        for i, (src, dst) in enumerate(((pair_hbm, pair), (coup_hbm, coup), (tgt_hbm, tgt)))
    ]
    own = pltpu.make_async_copy(pts_hbm, gathered.at[me], own_sem)
    barrier = pltpu.get_barrier_semaphore()
    for k in range(1, n):
        pl.semaphore_signal(
            barrier, inc=1, device_id=(group, (me + k) % n), device_id_type=MESH
        )
    small[0].start()
    small[1].start()
    own.start()
    for load in loads:
        load.start()
    small[2].start()

    small[0].wait()
    small[1].wait()
    label = lax.broadcasted_iota(jnp.int32, (PAIRS, blocks), 0)
    block_onehot = (label == pair[...]).astype(jnp.bfloat16)
    first = lax.broadcasted_iota(jnp.int32, (PAIRS, points), 0) * per_pair
    point = lax.broadcasted_iota(jnp.int32, (PAIRS, points), 1)
    point_onehot = ((point >= first) & (point < first + per_pair)).astype(jnp.bfloat16)
    links = jnp.dot(
        coup[...].astype(jnp.bfloat16), point_onehot, preferred_element_type=jnp.float32
    )
    mask = lax.dot_general(
        block_onehot,
        links.astype(jnp.bfloat16),
        (((0,), (0,)), ((), ())),
        preferred_element_type=jnp.float32,
    )
    pl.semaphore_wait(barrier, n - 1)

    sent = []

    def send(source, c, target, from_own):
        here = pl.ds(c * piece, piece)
        src = pts_hbm.at[here] if from_own else gathered.at[source, here]
        copy = pltpu.make_async_remote_copy(
            src_ref=src,
            dst_ref=gathered.at[source, here],
            send_sem=send_sem.at[len(sent)],
            recv_sem=recv_sem.at[source, c],
            device_id=(group, target),
            device_id_type=MESH,
        )
        copy.start()
        sent.append(copy)

    def arrived(source, c):
        here = pl.ds(c * piece, piece)
        pltpu.make_async_remote_copy(
            src_ref=gathered.at[source, here],
            dst_ref=gathered.at[source, here],
            send_sem=send_sem.at[0],
            recv_sem=recv_sem.at[source, c],
            device_id=(group, (me + 1) % n),
            device_id_type=MESH,
        ).wait_recv()

    partner = index(row, col, 1 - core)
    for c in range(CHUNKS):
        for k in range(1, outer):
            send(me, c, index((row + k) % outer, col, core), True)
        for k in range(1, inner):
            send(me, c, index(row, (col + k) % inner, core), True)
        send(me, c, partner, True)

    def relay(c):
        for k in range(1, outer):
            source = index((row + k) % outer, col, core)
            arrived(source, c)
            for j in range(1, inner):
                send(source, c, index(row, (col + j) % inner, core), False)
            send(source, c, partner, False)
        for k in range(outer):
            for j in range(1, inner):
                source = index((row + k) % outer, (col + j) % inner, core)
                arrived(source, c)
                send(source, c, partner, False)

    def multiply(c):
        for r in range(outer):
            for j in range(inner):
                arrived(index((row + r) % outer, (col + j) % inner, 1 - core), c)
        got = gathered[:, pl.ds(c * piece, piece), :].astype(jnp.float32)
        columns = []
        for t in range(tiles):
            columns.append(
                jnp.concatenate(
                    [got[d, t * pts_dev : (t + 1) * pts_dev, :] for d in range(n)], axis=0
                )
            )
        weights = jnp.concatenate(columns, axis=1).astype(jnp.bfloat16)
        loads[c].wait()
        dots = lax.dot_general(
            env[c], weights, (((1,), (1,)), ((), ())), preferred_element_type=jnp.float32
        )
        if c == 0:
            acc[...] = dots
        elif c < CHUNKS - 1:
            acc[...] += dots
        else:
            return acc[...] + dots

    own.wait()
    relay(0)
    for c in range(1, CHUNKS):
        relay(c)
        multiply(c - 1)
    dots = multiply(CHUNKS - 1).reshape(blocks, EBLK, points)
    values = (mask[:, None, :] * dots * dots).reshape(rows, points).astype(jnp.bfloat16)
    small[2].wait()
    gram = lax.dot_general(
        values, values, (((0,), (0,)), ((), ())), preferred_element_type=jnp.float32
    )
    proj = lax.dot_general(
        values, tgt[...], (((0,), (1,)), ((), ())), preferred_element_type=jnp.float32
    )
    part[:, :, :points] = gram.reshape(n, pts_dev, points)
    part[:, :, points : points + heads] = proj.reshape(n, pts_dev, heads)
    parts = []
    for k in range(1, n):
        target = (me + k) % n
        copy = pltpu.make_async_remote_copy(
            src_ref=part.at[target],
            dst_ref=landed.at[me],
            send_sem=part_send.at[k],
            recv_sem=part_recv.at[me],
            device_id=(group, target),
            device_id_type=MESH,
        )
        copy.start()
        parts.append(copy)
    landed[me] = part[me]
    for copy in sent:
        copy.wait_send()
    for k in range(1, n):
        source = (me + k) % n
        pltpu.make_async_remote_copy(
            src_ref=part.at[source],
            dst_ref=landed.at[source],
            send_sem=part_send.at[k],
            recv_sem=part_recv.at[source],
            device_id=(group, source),
            device_id_type=MESH,
        ).wait_recv()
    out_ref[...] = jnp.sum(landed[...], axis=0) / (rows * n)
    for copy in parts:
        copy.wait_send()


def shards(n, environments, targets, sparse_points, block_pair, coupling):
    rows, depth = environments.shape
    pts_dev = sparse_points.shape[0]
    points = pts_dev * n
    heads = targets.shape[0]
    blocks = block_pair.shape[0]
    outer, inner = grid_of(n)
    across = pl.cdiv(points + heads, LANES) * LANES
    flat = (
        sparse_points.reshape(pts_dev, depth // LANES, LANES)
        .transpose(1, 0, 2)
        .reshape(pts_dev * depth // LANES, LANES)
    )
    sends = CHUNKS * (outer - 1 + inner - 1 + 1 + (outer - 1) * inner + outer * (inner - 1))
    sums = pl.pallas_call(
        functools.partial(kernel, n),
        out_shape=jax.ShapeDtypeStruct((pts_dev, across), jnp.float32),
        in_specs=[pl.BlockSpec(memory_space=pl.ANY)] * 5,
        out_specs=pl.BlockSpec(memory_space=pltpu.VMEM),
        scratch_shapes=[
            pltpu.VMEM((CHUNKS, rows, depth // CHUNKS), jnp.bfloat16),
            pltpu.VMEM((heads, rows), jnp.bfloat16),
            pltpu.VMEM((1, blocks), jnp.int32),
            pltpu.VMEM((PAIRS, PAIRS), jnp.int32),
            pltpu.VMEM((n,) + flat.shape, jnp.bfloat16),
            pltpu.VMEM((rows, points), jnp.float32),
            pltpu.VMEM((n, pts_dev, across), jnp.float32),
            pltpu.VMEM((n, pts_dev, across), jnp.float32),
            pltpu.SemaphoreType.DMA((CHUNKS,)),
            pltpu.SemaphoreType.DMA((3,)),
            pltpu.SemaphoreType.DMA,
            pltpu.SemaphoreType.DMA((sends,)),
            pltpu.SemaphoreType.DMA((n, CHUNKS)),
            pltpu.SemaphoreType.DMA((n,)),
            pltpu.SemaphoreType.DMA((n,)),
        ],
        compiler_params=pltpu.CompilerParams(
            collective_id=0, has_side_effects=True, vmem_limit_bytes=48 * 2**20
        ),
        name="normal_equations",
    )(environments, targets, flat, block_pair.reshape(1, blocks), coupling)
    return sums[:, :points], sums[:, points : points + heads].T


def solution(mesh):
    in_specs = (
        P(("groups", "blk"), None),
        P(None, ("groups", "blk")),
        P(("groups", "blk"), None),
        P(("groups", "blk")),
        P(),
    )
    out_specs = (P(("groups", "blk"), None), P(None, ("groups", "blk")))
    return jax.shard_map(
        functools.partial(shards, mesh.shape["blk"]),
        mesh=mesh,
        in_specs=in_specs,
        out_specs=out_specs,
        check_vma=False,
    )
```

time: 94.5 us -> 36.4 us (0.39)
  blocking collectives: 82.7 us -> 0 us
  Pallas kernels: 0 us -> 31.4 us
  matrix products: 8.1 us -> 0 us
  local copies, waits for them, and re-layouts: 0.88 us -> 4.11 us
  other arithmetic: 1.24 us -> 0 us
    unnamed x1 -> x0, blocking collectives: 57.9 us -> none
    pallas_call x0 -> x1, Pallas kernels: none -> 31.4 us  [shards(): pl.pallas_call(functools.partial(kernel, n), out_shape=jax.ShapeDtypeStru...]
    all_gather x1 -> x0, blocking collectives: 24.8 us -> none  [shards(): piece = lax.all_gather(sparse_points, 'blk', axis=0, tiled=True)]
    dot_general x4 -> x0, matrix products: 8.1 us -> none  [the longest x1 7.28 us: shards(): lax.dot_general(environments, piece, (((1,), (1,)), ((), ())), preferred_...]
    unnamed x10, local copies, waits for them, and re-layouts: 0.73 us -> 4.04 us
    div x2 -> x0, other arithmetic: 1.23 us -> none  [shards(): return (own_gram / total, own_proj / total)]
where the time goes in v1:
time: 36.4 us; the launch traced here: 36.1 us
  Pallas kernels  31.4 us (86%)
  local copies, waits for them, and re-layouts  4.11 us (11%)
  between operations  0.65 us (2%)
    pallas_call x1, Pallas kernels, shards(): pl.pallas_call(functools.partial(kernel, n), out_shape=jax.ShapeDtypeStru...  31.4 us
    unnamed x10, local copies, waits for them, and re-layouts  4.04 us

profile of v1, /device:TPU:0, one launch (start us, length us, event | category | flops | bytes accessed | tf_op | source)
XLA Modules:
  0.0 36.1 jit_solution(4823102008953910531)
XLA Ops:
  0.6 0.0 copy-start
  0.6 0.7 %copy-done = bf16[4,4096]{1,0:T(4,128)(2,1)S(1)} copy-done((bf16[4,4096]{1,0:T(4,128)(2,1)S(1)}, bf16[4,4096]{1,0:T(4,128)(2,1)}, u32[]{:S(2)}) %copy-start) | copy-done | bytes 32792
  1.4 0.0 copy-start.1
  1.4 0.7 %copy-done.1 = bf16[3,1280]{1,0:T(4,128)(2,1)S(1)} copy-done((bf16[3,1280]{1,0:T(4,128)(2,1)S(1)}, bf16[3,1280]{1,0:T(4,128)(2,1)}, u32[]{:S(2)}) %copy-start.1) | copy-done | bytes 7704
  2.1 0.0 copy-start.2
  2.1 0.7 %copy-done.2 = s32[8,8]{1,0:T(8,128)S(1)} copy-done((s32[8,8]{1,0:T(8,128)S(1)}, s32[8,8]{1,0:T(8,128)}, u32[]{:S(2)}) %copy-start.2) | copy-done | bytes 280
  2.8 0.0 copy-start.3
  2.8 0.7 %copy-done.3 = s32[80]{0:T(128)S(1)} copy-done((s32[80]{0:T(128)S(1)}, s32[80]{0:T(128)}, u32[]{:S(2)}) %copy-start.3) | copy-done | bytes 344
  3.4 31.4 %normal_equations.1 = f32[4,128]{1,0:T(4,128)S(1)} custom-call(bf16[1280,4096]{1,0:T(8,128)(2,1)} %env_hbm.1, bf16[3,1280]{1,0:T(4,128)(2,1)S(1)} %copy-done.1, bf16[128,128]{1,0:T(8,128)(2,1)S(1)} %bitcast.9, s32[1,80]{1,0:T(1,128)S(1)} %bitcast.11, s32[8,8]{1,0:T(8,128)S(1)} %copy-done.2), custom_call_target="tpu_custom_call" | custom-call | tf_op jit(solution)/shard_map/normal_equations/pallas_call | solution.py:240
  34.8 0.1 slice_bitcast_fusion
  34.9 0.7 %copy.8 = f32[3,4]{1,0:T(4,128)} copy(f32[3,4]{0,1:T(4,128)S(1)} %slice_bitcast_fusion) | data formatting | bytes 96
  35.5 0.6 %copy.10 = f32[4,64]{1,0:T(4,128)} copy(f32[4,64]{1,0:T(4,128)S(1)} %bitcast.10) | data formatting | bytes 2048
Async XLA Ops:
  0.6 0.8 %copy-start = (bf16[4,4096]{1,0:T(4,128)(2,1)S(1)}, bf16[4,4096]{1,0:T(4,128)(2,1)}, u32[]{:S(2)}) copy-start(bf16[4,4096]{1,0:T(4,128)(2,1)} %param.7) | copy-start | bytes 98308
  1.4 0.7 %copy-start.1 = (bf16[3,1280]{1,0:T(4,128)(2,1)S(1)}, bf16[3,1280]{1,0:T(4,128)(2,1)}, u32[]{:S(2)}) copy-start(bf16[3,1280]{1,0:T(4,128)(2,1)} %tgt_hbm.1) | copy-start | bytes 23044
  2.1 0.7 %copy-start.2 = (s32[8,8]{1,0:T(8,128)S(1)}, s32[8,8]{1,0:T(8,128)}, u32[]{:S(2)}) copy-start(s32[8,8]{1,0:T(8,128)} %coup_hbm.1) | copy-start | bytes 772
  2.8 0.7 %copy-start.3 = (s32[80]{0:T(128)S(1)}, s32[80]{0:T(128)}, u32[]{:S(2)}) copy-start(s32[80]{0:T(128)} %param.8) | copy-start | bytes 964

commit v2 on v1

v2 whole, which is shorter than its diff:
```python
import functools

import jax
import jax.numpy as jnp
from jax import lax
from jax.experimental import pallas as pl
from jax.experimental.pallas import tpu as pltpu
from jax.sharding import PartitionSpec as P

EBLK = 16
PAIRS = 8
LANES = 128
LEGS = 1
CHUNKS = LEGS
VMEM_BYTES = 63 * 2**20
MESH = pl.DeviceIdType.MESH


def grid_of(devices):
    chips = devices // 2
    inner = 1
    while (inner * 2) ** 2 <= chips and chips % (inner * 2) == 0:
        inner *= 2
    return chips // inner, inner


def kernel(
    n,
    env_hbm,
    tgt_hbm,
    pts_hbm,
    pair_hbm,
    coup_hbm,
    out_ref,
    env,
    tgt,
    pair,
    coup,
    gathered,
    acc,
    part,
    landed,
    env_sem,
    small_sem,
    own_sem,
    send_sem,
    recv_sem,
    part_send,
    part_recv,
):
    outer, inner = grid_of(n)
    group = lax.axis_index("groups")
    me = lax.axis_index("blk")
    core = lax.rem(me, 2)
    chip = lax.div(me, 2)
    row = lax.div(chip, inner)
    col = lax.rem(chip, inner)
    plane = outer * inner
    rows = env_hbm.shape[0]
    width = env_hbm.shape[1] // CHUNKS
    piece = pts_hbm.shape[0] // CHUNKS
    leg = pts_hbm.shape[0] // LEGS
    tiles = width // LANES
    pts_dev = pts_hbm.shape[0] * LANES // env_hbm.shape[1]
    points = pts_dev * n
    per_pair = points // PAIRS
    heads = tgt_hbm.shape[0]
    blocks = rows // EBLK

    def index(r, c, k):
        return (r * inner + c) * 2 + k

    def slot(r, c, k):
        return (k * inner + c) * outer + r

    def other(k):
        return lax.rem(me + k, n)

    loads = [
        pltpu.make_async_copy(env_hbm.at[:, pl.ds(c * width, width)], env.at[c], env_sem.at[c])
        for c in range(CHUNKS)
    ]
    small = [
        pltpu.make_async_copy(src, dst, small_sem.at[i])
        for i, (src, dst) in enumerate(((pair_hbm, pair), (coup_hbm, coup), (tgt_hbm, tgt)))
    ]
    own = pltpu.make_async_copy(pts_hbm, gathered.at[slot(row, col, core)], own_sem)
    barrier = pltpu.get_barrier_semaphore()
    for k in range(1, n):
        pl.semaphore_signal(
            barrier, inc=1, device_id=(group, other(k)), device_id_type=MESH
        )
    small[0].start()
    small[1].start()
    own.start()
    for load in loads:
        load.start()
    small[2].start()

    pl.semaphore_wait(barrier, n - 1)

    def copy(first, count, c, target, sem):
        block = gathered.at[pl.ds(first, count), pl.ds(c * leg, leg)]
        return pltpu.make_async_remote_copy(
            src_ref=block,
            dst_ref=block,
            send_sem=send_sem,
            recv_sem=recv_sem.at[sem, c],
            device_id=(group, target),
            device_id_type=MESH,
        )

    partner = index(row, col, 1 - core)
    mine = slot(row, col, core)
    down = [lax.rem(row + k, outer) for k in range(outer)]
    aside = [lax.rem(col + k, inner) for k in range(inner)]
    own.wait()
    for c in range(LEGS):
        for j in range(inner):
            for k in range(outer):
                if j + k:
                    copy(mine, 1, c, index(down[k], aside[j], core), mine).start()

    def relay(c):
        for j in range(inner):
            for k in range(outer):
                if j + k:
                    source = slot(down[k], aside[j], core)
                    copy(source, 1, c, me, source).wait_recv()
            copy(slot(0, aside[j], core), outer, c, partner, n + aside[j]).start()

    def settle(c):
        for j in range(inner):
            copy(slot(0, aside[j], 1 - core), outer, c, me, n + aside[j]).wait_recv()

    small[0].wait()
    small[1].wait()
    label = lax.broadcasted_iota(jnp.int32, (PAIRS, blocks), 0)
    block_onehot = (label == pair[...]).astype(jnp.bfloat16)
    first = lax.broadcasted_iota(jnp.int32, (PAIRS, points), 0) * per_pair
    point = lax.broadcasted_iota(jnp.int32, (PAIRS, points), 1)
    point_onehot = ((point >= first) & (point < first + per_pair)).astype(jnp.bfloat16)
    links = jnp.dot(
        coup[...].astype(jnp.bfloat16), point_onehot, preferred_element_type=jnp.float32
    )
    mask = lax.dot_general(
        block_onehot,
        links.astype(jnp.bfloat16),
        (((0,), (0,)), ((), ())),
        preferred_element_type=jnp.float32,
    )

    def multiply(c):
        if c == 0:
            for load in loads:
                load.wait()
        got = gathered[:, pl.ds(c * piece, piece), :].astype(jnp.float32)
        columns = []
        for t in range(tiles):
            columns.append(
                jnp.concatenate(
                    [got[slot(r, j, k), t * pts_dev : (t + 1) * pts_dev, :]
                     for r in range(outer) for j in range(inner) for k in range(2)], axis=0
                )
            )
        weights = jnp.concatenate(columns, axis=1).astype(jnp.bfloat16)
        dots = lax.dot_general(
            env[c], weights, (((1,), (1,)), ((), ())), preferred_element_type=jnp.float32
        )
        if CHUNKS == 1:
            return dots
        if c == 0:
            acc[...] = dots
        elif c < CHUNKS - 1:
            acc[...] += dots
        else:
            return acc[...] + dots

    done = 0
    for c in range(LEGS):
        relay(c)
        if c:
            settle(c - 1)
            while (done + 1) * LEGS <= c * CHUNKS:
                multiply(done)
                done += 1
    settle(LEGS - 1)
    while done < CHUNKS:
        dots = multiply(done)
        done += 1
    dots = dots.reshape(blocks, EBLK, points)
    values = (mask[:, None, :] * dots * dots).reshape(rows, points).astype(jnp.bfloat16)
    small[2].wait()
    gram = lax.dot_general(
        values, values, (((0,), (0,)), ((), ())), preferred_element_type=jnp.float32
    )
    proj = lax.dot_general(
        values, tgt[...], (((0,), (1,)), ((), ())), preferred_element_type=jnp.float32
    )
    part[:, :, :points] = gram.reshape(n, pts_dev, points)
    part[:, :, points : points + heads] = proj.reshape(n, pts_dev, heads)
    for k in range(1, n):
        pltpu.make_async_remote_copy(
            src_ref=part.at[other(k)],
            dst_ref=landed.at[me],
            send_sem=part_send,
            recv_sem=part_recv,
            device_id=(group, other(k)),
            device_id_type=MESH,
        ).start()
    landed[me] = part[me]
    others = landed.at[pl.ds(0, n - 1)]
    sums = pltpu.make_async_remote_copy(
        src_ref=others,
        dst_ref=others,
        send_sem=part_send,
        recv_sem=part_recv,
        device_id=(group, other(1)),
        device_id_type=MESH,
    )
    sums.wait_recv()
    out_ref[...] = jnp.sum(landed[...], axis=0) / (rows * n)
    sums.wait_send()
    pltpu.make_async_remote_copy(
        src_ref=gathered.at[pl.ds(0, n - 1)],
        dst_ref=gathered.at[pl.ds(0, n - 1)],
        send_sem=send_sem,
        recv_sem=recv_sem.at[0, 0],
        device_id=(group, other(1)),
        device_id_type=MESH,
    ).wait_send()


def split(sums_ref, gram_ref, proj_ref):
    points = gram_ref.shape[1]
    heads = proj_ref.shape[0]
    gram_ref[...] = sums_ref[:, :points]
    proj_ref[...] = sums_ref[:, points : points + heads].T


def shards(n, environments, targets, sparse_points, block_pair, coupling):
    rows, depth = environments.shape
    pts_dev = sparse_points.shape[0]
    points = pts_dev * n
    heads = targets.shape[0]
    blocks = block_pair.shape[0]
    outer, inner = grid_of(n)
    across = pl.cdiv(points + heads, LANES) * LANES
    flat = (
        sparse_points.reshape(pts_dev, depth // LANES, LANES)
        .transpose(1, 0, 2)
        .reshape(pts_dev * depth // LANES, LANES)
    )
    sums = pl.pallas_call(
        functools.partial(kernel, n),
        out_shape=jax.ShapeDtypeStruct((pts_dev, across), jnp.float32),
        in_specs=[pl.BlockSpec(memory_space=pltpu.HBM)] * 5,
        out_specs=pl.BlockSpec(memory_space=pltpu.VMEM),
        scratch_shapes=[
            pltpu.VMEM((CHUNKS, rows, depth // CHUNKS), jnp.bfloat16),
            pltpu.VMEM((heads, rows), jnp.bfloat16),
            pltpu.VMEM((1, blocks), jnp.int32),
            pltpu.VMEM((PAIRS, PAIRS), jnp.int32),
            pltpu.VMEM((n,) + flat.shape, jnp.bfloat16),
            pltpu.VMEM((rows, points), jnp.float32),
            pltpu.VMEM((n, pts_dev, across), jnp.float32),
            pltpu.VMEM((n, pts_dev, across), jnp.float32),
            pltpu.SemaphoreType.DMA((CHUNKS,)),
            pltpu.SemaphoreType.DMA((3,)),
            pltpu.SemaphoreType.DMA,
            pltpu.SemaphoreType.DMA,
            pltpu.SemaphoreType.DMA((n + inner, LEGS)),
            pltpu.SemaphoreType.DMA,
            pltpu.SemaphoreType.DMA,
        ],
        compiler_params=pltpu.CompilerParams(
            collective_id=0, has_side_effects=True, vmem_limit_bytes=VMEM_BYTES
        ),
        name="normal_equations",
    )(environments, targets, flat, block_pair.reshape(1, blocks), coupling)
    return pl.pallas_call(
        split,
        out_shape=(
            jax.ShapeDtypeStruct((pts_dev, points), jnp.float32),
            jax.ShapeDtypeStruct((heads, pts_dev), jnp.float32),
        ),
        in_specs=[pl.BlockSpec(memory_space=pltpu.VMEM)],
        out_specs=[pl.BlockSpec(memory_space=pltpu.VMEM)] * 2,
        name="outputs",
    )(sums)


def solution(mesh):
    in_specs = (
        P(("groups", "blk"), None),
        P(None, ("groups", "blk")),
        P(("groups", "blk"), None),
        P(("groups", "blk")),
        P(),
    )
    out_specs = (P(("groups", "blk"), None), P(None, ("groups", "blk")))
    return jax.shard_map(
        functools.partial(shards, mesh.shape["blk"]),
        mesh=mesh,
        in_specs=in_specs,
        out_specs=out_specs,
        check_vma=False,
    )
```

time: 36.4 us -> 25.2 us (0.69)
  Pallas kernels: 31.4 us -> 24.4 us
  local copies, waits for them, and re-layouts: 4.11 us -> 0 us
    pallas_call x1, Pallas kernels: 31.4 us -> 23 us  [shards(): pl.pallas_call(functools.partial(kernel, n), out_shape=jax.ShapeDtypeStru...]
    unnamed x10 -> x0, local copies, waits for them, and re-layouts: 4.04 us -> none
    pallas_call x0 -> x1, Pallas kernels: none -> 1.4 us  [shards(): pl.pallas_call(split, out_shape=(jax.ShapeDtypeStruct((pts_dev, points),...]
where the time goes in v2:
time: 25.2 us; the launch traced here: 25 us
  Pallas kernels  24.4 us (97%)
  between operations  0.64 us (3%)
    pallas_call x1, Pallas kernels, shards(): pl.pallas_call(functools.partial(kernel, n), out_shape=jax.ShapeDtypeStru...  23 us
    pallas_call x1, Pallas kernels, shards(): pl.pallas_call(split, out_shape=(jax.ShapeDtypeStruct((pts_dev, points),...  1.4 us

profile of v2, /device:TPU:0, one launch (start us, length us, event | category | flops | bytes accessed | tf_op | source)
XLA Modules:
  0.0 25.0 jit_solution(9807182558508268287)
XLA Ops:
  0.6 23.0 %normal_equations.1.sums_ref = f32[4,128]{1,0:T(4,128)} custom-call(bf16[1280,4096]{1,0:T(8,128)(2,1)} %env_hbm.1, bf16[3,1280]{1,0:T(4,128)(2,1)} %tgt_hbm.1, bf16[128,128]{1,0:T(8,128)(2,1)} %bitcast.6, s32[1,80]{1,0:T(1,128)} %bitcast.7, s32[8,8]{1,0:T(8,128)} %coup_hbm.1), custom_call_target="tpu_custom_call" | custom-call | tf_op jit(solution)/shard_map/normal_equations/pallas_call | solution.py:254
  23.6 1.4 %outputs.1 = (f32[4,64]{1,0:T(4,128)}, f32[3,4]{1,0:T(4,128)}) custom-call(f32[4,128]{1,0:T(4,128)} %normal_equations.1.sums_ref), custom_call_target="tpu_custom_call" | custom-call | tf_op jit(solution)/shard_map/outputs/pallas_call | solution.py:281

commit v3 on v2

--- a/solution.py
+++ b/solution.py
@@ -10,8 +10,9 @@
 EBLK = 16
 PAIRS = 8
 LANES = 128
-LEGS = 1
-CHUNKS = LEGS
+LEGS = 2
+RELAYED = 3
+CHUNKS = 1
 VMEM_BYTES = 63 * 2**20
 MESH = pl.DeviceIdType.MESH
 
@@ -59,7 +60,7 @@
     rows = env_hbm.shape[0]
     width = env_hbm.shape[1] // CHUNKS
     piece = pts_hbm.shape[0] // CHUNKS
-    leg = pts_hbm.shape[0] // LEGS
+    leg = pts_hbm.shape[0] * RELAYED // 8
     tiles = width // LANES
     pts_dev = pts_hbm.shape[0] * LANES // env_hbm.shape[1]
     points = pts_dev * n
@@ -100,7 +101,7 @@
     pl.semaphore_wait(barrier, n - 1)
 
     def copy(first, count, c, target, sem):
-        block = gathered.at[pl.ds(first, count), pl.ds(c * leg, leg)]
+        block = gathered.at[pl.ds(first, count), pl.ds(c * leg, pts_hbm.shape[0] - leg if c else leg)]
         return pltpu.make_async_remote_copy(
             src_ref=block,
             dst_ref=block,
@@ -112,26 +113,17 @@
 
     partner = index(row, col, 1 - core)
     mine = slot(row, col, core)
-    down = [lax.rem(row + k, outer) for k in range(outer)]
+    down = [row] + [outer - 1 - t - lax.div(row + t + 1, outer) for t in range(outer - 1)]
     aside = [lax.rem(col + k, inner) for k in range(inner)]
     own.wait()
-    for c in range(LEGS):
+    for k in range(1, outer):
+        copy(mine, 1, 0, index(down[k], col, core), mine).start()
+    for j in range(1, inner):
+        copy(mine, 1, 0, index(row, aside[j], core), mine).start()
+    for k in [*range(1, outer), 0]:
         for j in range(inner):
-            for k in range(outer):
-                if j + k:
-                    copy(mine, 1, c, index(down[k], aside[j], core), mine).start()
-
-    def relay(c):
-        for j in range(inner):
-            for k in range(outer):
-                if j + k:
-                    source = slot(down[k], aside[j], core)
-                    copy(source, 1, c, me, source).wait_recv()
-            copy(slot(0, aside[j], core), outer, c, partner, n + aside[j]).start()
-
-    def settle(c):
-        for j in range(inner):
-            copy(slot(0, aside[j], 1 - core), outer, c, me, n + aside[j]).wait_recv()
+            if j + k:
+                copy(mine, 1, 1, index(down[k], aside[j], core), mine).start()
 
     small[0].wait()
     small[1].wait()
@@ -176,18 +168,26 @@
         else:
             return acc[...] + dots
 
-    done = 0
-    for c in range(LEGS):
-        relay(c)
-        if c:
-            settle(c - 1)
-            while (done + 1) * LEGS <= c * CHUNKS:
-                multiply(done)
-                done += 1
-    settle(LEGS - 1)
-    while done < CHUNKS:
-        dots = multiply(done)
-        done += 1
+    for k in range(1, outer):
+        source = slot(down[k], col, core)
+        copy(source, 1, 0, me, source).wait_recv()
+        for j in range(1, inner):
+            copy(source, 1, 0, index(row, aside[j], core), source).start()
+    for j in range(1, inner):
+        for k in range(outer):
+            source = slot(down[k], aside[j], core)
+            copy(source, 1, 0, me, source).wait_recv()
+    here, there = slot(0, 0, core), slot(0, 0, 1 - core)
+    copy(here, plane, 0, partner, n).start()
+    for j in range(inner):
+        for k in range(outer):
+            if j + k:
+                source = slot(down[k], aside[j], core)
+                copy(source, 1, 1, me, source).wait_recv()
+    copy(here, plane, 1, partner, n).start()
+    copy(there, plane, 0, me, n).wait_recv()
+    copy(there, plane, 1, me, n).wait_recv()
+    dots = multiply(0)
     dots = dots.reshape(blocks, EBLK, points)
     values = (mask[:, None, :] * dots * dots).reshape(rows, points).astype(jnp.bfloat16)
     small[2].wait()
@@ -269,7 +269,7 @@
             pltpu.SemaphoreType.DMA((3,)),
             pltpu.SemaphoreType.DMA,
             pltpu.SemaphoreType.DMA,
-            pltpu.SemaphoreType.DMA((n + inner, LEGS)),
+            pltpu.SemaphoreType.DMA((n + 1, LEGS)),
             pltpu.SemaphoreType.DMA,
             pltpu.SemaphoreType.DMA,
         ],

time: 25.2 us -> 23.9 us (0.948)
  Pallas kernels: 24.4 us -> 23.1 us
    pallas_call x1, Pallas kernels: 23 us -> 21.7 us  [shards(): pl.pallas_call(functools.partial(kernel, n), out_shape=jax.ShapeDtypeStru...]
where the time goes in v3:
time: 23.9 us; the launch traced here: 23.7 us
  Pallas kernels  23.1 us (97%)
  between operations  0.64 us (3%)
    pallas_call x1, Pallas kernels, shards(): pl.pallas_call(functools.partial(kernel, n), out_shape=jax.ShapeDtypeStru...  21.7 us
    pallas_call x1, Pallas kernels, shards(): pl.pallas_call(split, out_shape=(jax.ShapeDtypeStruct((pts_dev, points),...  1.4 us

profile of v3, /device:TPU:0, one launch (start us, length us, event | category | flops | bytes accessed | tf_op | source)
XLA Modules:
  0.0 23.7 jit_solution(15341482662377728636)
XLA Ops:
  0.6 21.7 %normal_equations.1.sums_ref = f32[4,128]{1,0:T(4,128)} custom-call(bf16[1280,4096]{1,0:T(8,128)(2,1)} %env_hbm.1, bf16[3,1280]{1,0:T(4,128)(2,1)} %tgt_hbm.1, bf16[128,128]{1,0:T(8,128)(2,1)} %bitcast.6, s32[1,80]{1,0:T(1,128)} %bitcast.7, s32[8,8]{1,0:T(8,128)} %coup_hbm.1), custom_call_target="tpu_custom_call" | custom-call | tf_op jit(solution)/shard_map/normal_equations/pallas_call | solution.py:254
  22.3 1.4 %outputs.1 = (f32[4,64]{1,0:T(4,128)}, f32[3,4]{1,0:T(4,128)}) custom-call(f32[4,128]{1,0:T(4,128)} %normal_equations.1.sums_ref), custom_call_target="tpu_custom_call" | custom-call | tf_op jit(solution)/shard_map/outputs/pallas_call | solution.py:281

commit v4 on v3

--- a/solution.py
+++ b/solution.py
@@ -121,7 +121,7 @@
     for j in range(1, inner):
         copy(mine, 1, 0, index(row, aside[j], core), mine).start()
     for k in [*range(1, outer), 0]:
-        for j in range(inner):
+        for j in reversed(range(inner)):
             if j + k:
                 copy(mine, 1, 1, index(down[k], aside[j], core), mine).start()
 

time: 23.9 us -> 23.7 us (level)
  no operation moved by 1% of the time
where the time goes in v4:
time: 23.7 us; the launch traced here: 23.6 us
  Pallas kernels  22.9 us (97%)
  between operations  0.64 us (3%)
    pallas_call x1, Pallas kernels, shards(): pl.pallas_call(functools.partial(kernel, n), out_shape=jax.ShapeDtypeStru...  21.5 us
    pallas_call x1, Pallas kernels, shards(): pl.pallas_call(split, out_shape=(jax.ShapeDtypeStruct((pts_dev, points),...  1.4 us

profile of v4, /device:TPU:0, one launch (start us, length us, event | category | flops | bytes accessed | tf_op | source)
XLA Modules:
  0.0 23.6 jit_solution(6629563041835014545)
XLA Ops:
  0.6 21.5 %normal_equations.1.sums_ref = f32[4,128]{1,0:T(4,128)} custom-call(bf16[1280,4096]{1,0:T(8,128)(2,1)} %env_hbm.1, bf16[3,1280]{1,0:T(4,128)(2,1)} %tgt_hbm.1, bf16[128,128]{1,0:T(8,128)(2,1)} %bitcast.6, s32[1,80]{1,0:T(1,128)} %bitcast.7, s32[8,8]{1,0:T(8,128)} %coup_hbm.1), custom_call_target="tpu_custom_call" | custom-call | tf_op jit(solution)/shard_map/normal_equations/pallas_call | solution.py:254
  22.2 1.4 %outputs.1 = (f32[4,64]{1,0:T(4,128)}, f32[3,4]{1,0:T(4,128)}) custom-call(f32[4,128]{1,0:T(4,128)} %normal_equations.1.sums_ref), custom_call_target="tpu_custom_call" | custom-call | tf_op jit(solution)/shard_map/outputs/pallas_call | solution.py:281
